TPU v7x, 256 devices: a whole 4x4x8 slice. The times are simulated.
256 devices in a mesh: dp: 4 (over y), seq: 64 (over z, x, core).
Axes of the slice: x: 4, y: 4, z: 8, core: 2. Of those that a mesh axis runs over, the one named last changes fastest.
Arguments:
- query: bfloat16 [4, 16384, 1536], P('dp', 'seq'), may hold values from -6 to 6
- key: bfloat16 [4, 16384, 1536], P('dp', 'seq'), may hold values from -6 to 6
- value: bfloat16 [4, 16384, 1536], P('dp', 'seq'), may hold values from -6 to 6
- segments: int32 [4, 16384], P('dp', 'seq'), may hold values from 0 to 95, never falling along the last dimension, each value on 1 to 256 neighbouring positions
- out_proj: bfloat16 [1536, 1536], replicated, may hold values from -0.15625 to 0.15625
- conv_kernel: bfloat16 [31, 1536], replicated, may hold values from -1 to 1
- cotangent: bfloat16 [4, 16384, 1536], P('dp', 'seq'), may hold values from -6 to 6
Outputs:
- block_out: bfloat16 [4, 16384, 1536], P('dp', 'seq')
- grad_query: bfloat16 [4, 16384, 1536], P('dp', 'seq')
- grad_key: bfloat16 [4, 16384, 1536], P('dp', 'seq')
- grad_value: bfloat16 [4, 16384, 1536], P('dp', 'seq')
- grad_kernel: float32 [31, 1536], replicated
- grad_out_proj: float32 [1536, 1536], P(('dp', 'seq'))
Inputs may be any that keep to these rules, and one draw needn't show every extreme that they name: `segments`: along the frames of a data group the utterance number never falls; every utterance holds 1 to 256 frames and one holds exactly 256.
All inputs are finite; a program needn't handle non-finite values.
Results may differ from a plain program's by a relative error of at most 0.02.
Values may be sent and summed in bfloat16 or wider, within the bound.
No kernel may reach another device: no remote copies, remote signals or barrier semaphores. Data moves between devices by JAX's collectives and lax.ppermute only.
A program may use at most 128 MiB of HBM per device.

v0:
```python
import jax
import jax.numpy as jnp
from jax import lax
from jax.sharding import PartitionSpec as P

HD = 64
KW = 31


def extended(block, sides, width):
    for axis, dim in sides:
        count = lax.axis_size(axis)
        forward = [(i, i + 1) for i in range(count - 1)]
        backward = [(target, source) for source, target in forward]
        low = lax.ppermute(
            lax.slice_in_dim(block, block.shape[dim] - width, None, axis=dim), axis, forward
        )
        high = lax.ppermute(lax.slice_in_dim(block, 0, width, axis=dim), axis, backward)
        block = jnp.concatenate([low, block, high], axis=dim)
    return block


def from_behind(value, axis, steps):
    count = lax.axis_size(axis)
    first, last = (max(0, -steps), min(count, count - steps))
    return lax.ppermute(value, axis, [(source, source + steps) for source in range(first, last)])


def head_scores(queries, keys_block, query_ids, key_ids):
    query_heads = queries.reshape(queries.shape[0], -1, HD)
    key_heads = keys_block.reshape(keys_block.shape[0], -1, HD)
    scores = jnp.einsum(
        "rhe,whe->hrw", query_heads, key_heads, preferred_element_type=jnp.float32
    ) * HD ** (-0.5)
    allowed = query_ids[:, None] == key_ids[None, :]
    return jnp.where(allowed[None], scores, -1e30)


def to_groups(matrix):
    return jnp.moveaxis(matrix.reshape(matrix.shape[0], -1, 4 * HD), 1, 0)


def from_groups(stacked):
    return jnp.moveaxis(stacked, 0, 1).reshape(stacked.shape[1], -1)


def attend(queries, keys_block, values_block, query_ids, key_ids):
    scores = head_scores(queries, keys_block, query_ids, key_ids)
    highest = jnp.max(scores, axis=2)
    weights = jnp.exp(scores - highest[:, :, None])
    totals = jnp.sum(weights, axis=2)
    probs = (weights / totals[:, :, None]).astype(jnp.bfloat16)
    value_heads = values_block.reshape(values_block.shape[0], -1, HD)
    context = jnp.einsum("hrw,whe->rhe", probs, value_heads, preferred_element_type=jnp.float32)
    return (context.reshape(queries.shape[0], -1), highest, totals)


def score_grads(
    queries, keys_block, values_block, upstream, highest, totals, deltas, query_ids, key_ids
):
    scores = head_scores(queries, keys_block, query_ids, key_ids)
    probs = jnp.exp(scores - highest[:, :, None]) / totals[:, :, None]
    upstream_heads = upstream.reshape(upstream.shape[0], -1, HD)
    value_heads = values_block.reshape(values_block.shape[0], -1, HD)
    prob_grads = jnp.einsum(
        "rhe,whe->hrw", upstream_heads, value_heads, preferred_element_type=jnp.float32
    )
    score_grad = (probs * (prob_grads - deltas[:, :, None]) * HD ** (-0.5)).astype(jnp.bfloat16)
    return (probs.astype(jnp.bfloat16), score_grad, upstream_heads)


def query_side(queries, keys_block, score_grad):
    key_heads = keys_block.reshape(keys_block.shape[0], -1, HD)
    grads = jnp.einsum("hrw,whe->rhe", score_grad, key_heads, preferred_element_type=jnp.float32)
    return grads.reshape(queries.shape[0], -1)


def key_side(queries, keys_block, probs, score_grad, upstream_heads):
    query_heads = queries.reshape(queries.shape[0], -1, HD)
    key_part = jnp.einsum(
        "hrw,rhe->whe", score_grad, query_heads, preferred_element_type=jnp.float32
    )
    value_part = jnp.einsum(
        "hrw,rhe->whe", probs, upstream_heads, preferred_element_type=jnp.float32
    )
    return (key_part.reshape(keys_block.shape[0], -1), value_part.reshape(keys_block.shape[0], -1))


def per_device(query, key, value, segments, out_proj, conv_kernel, cotangent):
    frame_count = query.shape[1]
    width = query.shape[2]
    group_count = width // (4 * HD)
    reach = KW // 2
    queries = query[0]
    keys_local = key[0]
    values_local = value[0]
    own_ids = segments[0] + 1
    wide_ids = extended(own_ids, (("seq", 0),), frame_count)
    paired = extended(jnp.stack([keys_local, values_local]), (("seq", 1),), frame_count)

    def forward_group(items):
        return attend(items[0], items[1], items[2], own_ids, wide_ids)

    context_groups, highest, totals = lax.map(
        forward_group, (to_groups(queries), to_groups(paired[0]), to_groups(paired[1]))
    )
    context = from_groups(context_groups)
    context_b = context.astype(jnp.bfloat16)
    attended = jnp.dot(context_b, out_proj, preferred_element_type=jnp.float32).astype(jnp.bfloat16)
    attended_wide = extended(attended, (("seq", 0),), reach)
    conv_ids = wide_ids[frame_count - reach : 2 * frame_count + reach]
    kernel = conv_kernel.astype(jnp.float32)
    masks = [(conv_ids[offset : offset + frame_count] == own_ids)[:, None] for offset in range(KW)]
    convolved = jnp.zeros((frame_count, width), jnp.float32)
    for offset in range(KW):
        convolved = convolved + jnp.where(
            masks[offset],
            kernel[offset] * attended_wide[offset : offset + frame_count].astype(jnp.float32),
            0.0,
        )
    gate = jax.nn.sigmoid(convolved)
    block_out = (convolved * gate).astype(jnp.bfloat16)
    conv_grad = (cotangent[0].astype(jnp.float32) * gate * (1.0 + convolved * (1.0 - gate))).astype(
        jnp.bfloat16
    )
    conv_grad_wide = extended(conv_grad, (("seq", 0),), reach)
    conv_grad_f = conv_grad.astype(jnp.float32)
    attended_grad = jnp.zeros((frame_count, width), jnp.float32)
    kernel_rows = []
    for offset in range(KW):
        mirror = 2 * reach - offset
        attended_grad = attended_grad + jnp.where(
            masks[mirror],
            kernel[offset] * conv_grad_wide[mirror : mirror + frame_count].astype(jnp.float32),
            0.0,
        )
        kernel_rows.append(
            jnp.sum(
                jnp.where(
                    masks[offset],
                    conv_grad_f * attended_wide[offset : offset + frame_count].astype(jnp.float32),
                    0.0,
                ),
                axis=0,
            )
        )
    scale_out = (lax.axis_size("dp") * lax.axis_size("seq") * frame_count) ** (-0.5)
    grad_kernel = lax.psum(jnp.stack(kernel_rows), ("dp", "seq")) * scale_out
    attended_grad_b = attended_grad.astype(jnp.bfloat16)
    reduced = lax.psum_scatter(
        lax.dot_general(
            context_b, attended_grad_b, (((0,), (0,)), ((), ())), preferred_element_type=jnp.float32
        ),
        ("dp", "seq"),
        scatter_dimension=0,
        tiled=True,
    )
    grad_out_proj = reduced * scale_out
    context_grad = lax.dot_general(
        attended_grad_b, out_proj, (((1,), (1,)), ((), ())), preferred_element_type=jnp.float32
    ).astype(jnp.bfloat16)
    products = (to_groups(context_grad).astype(jnp.float32) * to_groups(context)).reshape(
        group_count, frame_count, 4, HD
    )
    deltas = jnp.moveaxis(jnp.sum(products, axis=3), 2, 1)

    def both_group(items):
        probs, score_grad, upstream_heads = score_grads(
            items[0], items[1], items[2], items[3], items[4], items[5], items[6], own_ids, wide_ids
        )
        key_part, value_part = key_side(items[0], items[1], probs, score_grad, upstream_heads)
        return (query_side(items[0], items[1], score_grad), key_part, value_part)

    query_part, key_part, value_part = lax.map(
        both_group,
        (
            to_groups(queries),
            to_groups(paired[0]),
            to_groups(paired[1]),
            to_groups(context_grad),
            highest,
            totals,
            deltas,
        ),
    )
    key_wide = from_groups(key_part)
    value_wide = from_groups(value_part)
    earlier = jnp.stack([key_wide[:frame_count], value_wide[:frame_count]])
    later = jnp.stack([key_wide[2 * frame_count :], value_wide[2 * frame_count :]])
    from_later = from_behind(earlier.astype(jnp.bfloat16), "seq", -1).astype(earlier.dtype)
    from_earlier = from_behind(later.astype(jnp.bfloat16), "seq", 1).astype(later.dtype)
    key_total = key_wide[frame_count : 2 * frame_count] + from_later[0] + from_earlier[0]
    value_total = value_wide[frame_count : 2 * frame_count] + from_later[1] + from_earlier[1]
    grad_query = from_groups(query_part).astype(jnp.bfloat16)
    grad_key = key_total.astype(jnp.bfloat16)
    grad_value = value_total.astype(jnp.bfloat16)
    return (
        block_out[None],
        grad_query[None],
        grad_key[None],
        grad_value[None],
        grad_kernel,
        grad_out_proj,
    )


def solution(mesh):
    in_specs = (
        P("dp", "seq", None),
        P("dp", "seq", None),
        P("dp", "seq", None),
        P("dp", "seq"),
        P(),
        P(),
        P("dp", "seq", None),
    )
    out_specs = (
        P("dp", "seq", None),
        P("dp", "seq", None),
        P("dp", "seq", None),
        P("dp", "seq", None),
        P(),
        P(("dp", "seq"), None),
    )
    return jax.shard_map(
        per_device, mesh=mesh, in_specs=in_specs, out_specs=out_specs, check_vma=False
    )
```

profile of v0, /device:TPU:1, one launch (start us, length us, event | category | flops | bytes accessed | tf_op | source)
XLA Modules:
  0.0 1732.6 jit_solution(641398557045694055)
XLA Ops:
  8.6 15.1 collective-permute-start.1
  30.7 13.3 collective-permute-start.3
  59.3 38.1 %while.30 = (s32[]{:T(128)}, f32[6,256,256]{1,2,0:T(8,128)}, f32[6,4,256]{2,1,0:T(4,128)}, f32[6,4,256]{2,1,0:T(4,128)}, bf16[6,768,256]{1,2,0:T(8,128)(2,1)S(1)...) while((s32[]{:T(128)}, f32[6,256,256]{1,2,0:T(8,128)}, ...), condition=%wide.region_3.4_spmd.clone, body=%wide.region_0.3_spmd.sunk.clone | while | flops 210958336 | bytes 13804649 | solution.py:104
  112.0 22.7 %fusion.142 = (f32[1536]{0:T(1024)}, f32[1536]{0:T(1024)}, f32[1536]{0:T(1024)}, f32[1536]{0:T(1024)}, f32[1536]{0:T(1024)}, /*index=5*/f32[1536]{0:T(1024)}, bf16[256,1536]{1,0:T(8,128)(2,1)S(1)}, f32[256,1536]{1,0:T(8,128)}) fusion(pred[256]{0:T(512)(128)(4,1)S(1)} %get-tuple-element.289, bf16[15,1536]{1,0:T(8,128)(2,1)S(1)} %collective-permute-done.5, ...), kind=kLoop, calls=%fused_computation.286 | loop fusion | flops 104193024 | bytes 4259328 | tf_op jit(solution)/shard_map/reduce_sum | solution.py:138
  142.5 24.2 %fusion.149 = bf16[256,1536]{1,0:T(8,128)(2,1)S(1)} fusion(bf16[256,1536]{1,0:T(8,128)(2,1)S(1)} %get-tuple-element.248, bf16[15,1536]{1,0:T(8,128)(2,1)} %collective-permute-done.7, bf16[15,1536]{1,0:T(8,128)(2,1)} %copy-done.74, f32[1536]{0:T(1024)S(1)} %get-tuple-element.174, f32[1536]{0:T(1024)S(1)} %get-tuple-element.175, ...), kind=kLoop, calls=%fused_computation.304 | loop fusion | flops 83755008 | bytes 1863168 | tf_op jit(solution)/shard_map/convert_element_type | solution.py:149
  171.8 723.4 %fusion = f32[8,1536]{1,0:T(8,128)S(1)} fusion(f32[1536,1536]{1,0:T(8,128)} %fusion.216), kind=kCustom, calls=%all-reduce-scatter | all-reduce-scatter fusion | flops 3145729 | bytes 9486336
  897.8 13.3 collective-permute-start.11
  930.9 13.1 collective-permute-start.13
  944.0 13.1 collective-permute-start.14
  957.2 13.1 collective-permute-start.15
  970.3 13.1 collective-permute-start.16
  1002.5 13.1 collective-permute-start.18
  1015.7 13.1 collective-permute-start.19
  1111.3 13.3 collective-permute-start.26
  1141.2 13.7 collective-permute-start.28
  1154.9 13.1 collective-permute-start.29
  1168.1 13.1 collective-permute-start.30
  1181.2 13.1 collective-permute-start.31
  1267.5 13.7 collective-permute-start.37
  1281.2 13.1 collective-permute-start.38
  1294.4 13.1 collective-permute-start.39
  1318.2 52.4 %while.31 = (s32[]{:T(128)}, bf16[6,256,256]{1,2,0:T(8,128)(2,1)S(1)}, f32[6,768,256]{1,2,0:T(8,128)}, f32[6,768,256]{1,2,0:T(8,128)}, bf16[6,768,256]{1,2,0:T(8...) while((s32[]{:T(128)}, ...), condition=%wide.region_6.7_spmd.clone, body=%wide.region_5.6_spmd.sunk.clone | while | flops 510590976 | bytes 23504016 | solution.py:174
  1489.9 96.9 %concatenate.118 = f32[518,1536]{1,0:T(8,128)} concatenate(f32[6,1536]{1,0:T(8,128)S(1)} %collective-permute-done.73, f32[8,1536]{1,0:T(8,128)} %collective-permute-done.72, f32[8,1536]{1,0:T(8,128)} %collective-permute-done.71, f32[8,1536]{1,0:T(8,128)} %collective-permute-done.70, f32[8,1536]{1,0:T(8,128)} %collective-permute-done.69, f32[8,1536]{1,0:T(8,128)} %collective-permute-done.68, ...), dimensions={0} | concatenate | bytes 6365184
  1588.4 128.7 %all-reduce.4.cloned.1.call-done = f32[31,1536]{1,0:T(8,128)} async-done(((f32[31,1536]{1,0:T(8,128)}), f32[31,1536]{1,0:T(8,128)}) %all-reduce.4.cloned.1.call-update) | async-done | bytes 190480 | tf_op jit(solution)/shard_map/psum | solution.py:148
  (664 shorter events, 491.5 us)
Async XLA Ops:
  7.2 1709.9 %all-reduce.4.cloned.1.call-start = ((), (), s32[]{:S(2)}) async-start(), calls=%async_computation | async-start | bytes 393216 | tf_op jit(solution)/shard_map/psum | solution.py:148
  897.8 72.5 %collective-permute-start.11 = (f32[8,1536]{1,0:T(8,128)S(1)}, f32[8,1536]{1,0:T(8,128)S(1)}, u32[]{:S(2)}, u32[]{:S(2)}) collective-permute-start(f32[8,1536]{1,0:T(8,128)S(1)} %fusion), channel_id=1, source_target_pairs={{0,2},{1,3},{2,4},{3,5},{4,6},{5,7},{6,8},{7,9},{8,10},{9,11},{10,... | collective-permute-start | bytes 147464
  917.8 71.6 %collective-permute-start.12 = (f32[8,1536]{1,0:T(8,128)S(1)}, f32[8,1536]{1,0:T(8,128)S(1)}, u32[]{:S(2)}, u32[]{:S(2)}) collective-permute-start(f32[8,1536]{1,0:T(8,128)S(1)} %fusion), channel_id=1, source_target_pairs={{0,3},{1,4},{2,5},{3,6},{4,7},{5,8},{6,9},{7,10},{8,11},{9,12},{10... | collective-permute-start | bytes 147464
  930.9 71.6 %collective-permute-start.13 = (f32[8,1536]{1,0:T(8,128)S(1)}, f32[8,1536]{1,0:T(8,128)S(1)}, u32[]{:S(2)}, u32[]{:S(2)}) collective-permute-start(f32[8,1536]{1,0:T(8,128)S(1)} %fusion), channel_id=1, source_target_pairs={{0,4},{1,5},{2,6},{3,7},{4,8},{5,9},{6,10},{7,11},{8,12},{9,13},{1... | collective-permute-start | bytes 147464
  944.0 71.6 %collective-permute-start.14 = (f32[8,1536]{1,0:T(8,128)S(1)}, f32[8,1536]{1,0:T(8,128)S(1)}, u32[]{:S(2)}, u32[]{:S(2)}) collective-permute-start(f32[8,1536]{1,0:T(8,128)S(1)} %fusion), channel_id=1, source_target_pairs={{0,5},{1,6},{2,7},{3,8},{4,9},{5,10},{6,11},{7,12},{8,13},{9,14},{... | collective-permute-start | bytes 147464
  957.2 71.7 %collective-permute-start.15 = (f32[8,1536]{1,0:T(8,128)S(1)}, f32[8,1536]{1,0:T(8,128)S(1)}, u32[]{:S(2)}, u32[]{:S(2)}) collective-permute-start(f32[8,1536]{1,0:T(8,128)S(1)} %fusion), channel_id=1, source_target_pairs={{0,6},{1,7},{2,8},{3,9},{4,10},{5,11},{6,12},{7,13},{8,14},{9,15},... | collective-permute-start | bytes 147464
  970.3 71.7 %collective-permute-start.16 = (f32[8,1536]{1,0:T(8,128)S(1)}, f32[8,1536]{1,0:T(8,128)S(1)}, u32[]{:S(2)}, u32[]{:S(2)}) collective-permute-start(f32[8,1536]{1,0:T(8,128)S(1)} %fusion), channel_id=1, source_target_pairs={{0,7},{1,8},{2,9},{3,10},{4,11},{5,12},{6,13},{7,14},{8,15},{9,16}... | collective-permute-start | bytes 147464
  989.4 69.4 %collective-permute-start.17 = (f32[8,1536]{1,0:T(8,128)S(1)}, f32[8,1536]{1,0:T(8,128)S(1)}, u32[]{:S(2)}, u32[]{:S(2)}) collective-permute-start(f32[8,1536]{1,0:T(8,128)S(1)} %fusion), channel_id=1, source_target_pairs={{0,8},{1,9},{2,10},{3,11},{4,12},{5,13},{6,14},{7,15},{8,16},{9,17... | collective-permute-start | bytes 147464
  1002.5 69.3 %collective-permute-start.18 = (f32[8,1536]{1,0:T(8,128)S(1)}, f32[8,1536]{1,0:T(8,128)S(1)}, u32[]{:S(2)}, u32[]{:S(2)}) collective-permute-start(f32[8,1536]{1,0:T(8,128)S(1)} %fusion), channel_id=1, source_target_pairs={{0,9},{1,10},{2,11},{3,12},{4,13},{5,14},{6,15},{7,16},{8,17},{9,1... | collective-permute-start | bytes 147464
  1085.0 69.9 %collective-permute-start.24 = (f32[8,1536]{1,0:T(8,128)S(1)}, f32[8,1536]{1,0:T(8,128)S(1)}, u32[]{:S(2)}, u32[]{:S(2)}) collective-permute-start(f32[8,1536]{1,0:T(8,128)S(1)} %fusion), channel_id=1, source_target_pairs={{0,15},{1,16},{2,17},{3,18},{4,19},{5,20},{6,21},{7,22},{8,23},{9,... | collective-permute-start | bytes 147464
  1098.2 69.9 %collective-permute-start.25 = (f32[8,1536]{1,0:T(8,128)S(1)}, f32[8,1536]{1,0:T(8,128)S(1)}, u32[]{:S(2)}, u32[]{:S(2)}) collective-permute-start(f32[8,1536]{1,0:T(8,128)S(1)} %fusion), channel_id=1, source_target_pairs={{0,16},{1,17},{2,18},{3,19},{4,20},{5,21},{6,22},{7,23},{8,24},{9,... | collective-permute-start | bytes 147464
  1111.3 69.9 %collective-permute-start.26 = (f32[8,1536]{1,0:T(8,128)S(1)}, f32[8,1536]{1,0:T(8,128)S(1)}, u32[]{:S(2)}, u32[]{:S(2)}) collective-permute-start(f32[8,1536]{1,0:T(8,128)S(1)} %fusion), channel_id=1, source_target_pairs={{0,17},{1,18},{2,19},{3,20},{4,21},{5,22},{6,23},{7,24},{8,25},{9,... | collective-permute-start | bytes 147464
  1128.1 72.5 %collective-permute-start.27 = (f32[8,1536]{1,0:T(8,128)S(1)}, f32[8,1536]{1,0:T(8,128)S(1)}, u32[]{:S(2)}, u32[]{:S(2)}) collective-permute-start(f32[8,1536]{1,0:T(8,128)S(1)} %fusion), channel_id=1, source_target_pairs={{0,18},{1,19},{2,20},{3,21},{4,22},{5,23},{6,24},{7,25},{8,26},{9,... | collective-permute-start | bytes 147464
  1141.2 72.0 %collective-permute-start.28 = (f32[8,1536]{1,0:T(8,128)S(1)}, f32[8,1536]{1,0:T(8,128)}, u32[]{:S(2)}, u32[]{:S(2)}) collective-permute-start(f32[8,1536]{1,0:T(8,128)S(1)} %fusion), channel_id=1, source_target_pairs={{0,19},{1,20},{2,21},{3,22},{4,23},{5,24},{6,25},{7,26},{8,27},{9,... | collective-permute-start | bytes 147464
  1154.9 71.4 %collective-permute-start.29 = (f32[8,1536]{1,0:T(8,128)S(1)}, f32[8,1536]{1,0:T(8,128)}, u32[]{:S(2)}, u32[]{:S(2)}) collective-permute-start(f32[8,1536]{1,0:T(8,128)S(1)} %fusion), channel_id=1, source_target_pairs={{0,20},{1,21},{2,22},{3,23},{4,24},{5,25},{6,26},{7,27},{8,28},{9,... | collective-permute-start | bytes 147464
  1168.1 71.4 %collective-permute-start.30 = (f32[8,1536]{1,0:T(8,128)S(1)}, f32[8,1536]{1,0:T(8,128)}, u32[]{:S(2)}, u32[]{:S(2)}) collective-permute-start(f32[8,1536]{1,0:T(8,128)S(1)} %fusion), channel_id=1, source_target_pairs={{0,21},{1,22},{2,23},{3,24},{4,25},{5,26},{6,27},{7,28},{8,29},{9,... | collective-permute-start | bytes 147464
  1181.2 71.4 %collective-permute-start.31 = (f32[8,1536]{1,0:T(8,128)S(1)}, f32[8,1536]{1,0:T(8,128)}, u32[]{:S(2)}, u32[]{:S(2)}) collective-permute-start(f32[8,1536]{1,0:T(8,128)S(1)} %fusion), channel_id=1, source_target_pairs={{0,22},{1,23},{2,24},{3,25},{4,26},{5,27},{6,28},{7,29},{8,30},{9,... | collective-permute-start | bytes 147464
  1267.5 103.1 %collective-permute-start.37 = (f32[8,1536]{1,0:T(8,128)S(1)}, f32[8,1536]{1,0:T(8,128)}, u32[]{:S(2)}, u32[]{:S(2)}) collective-permute-start(f32[8,1536]{1,0:T(8,128)S(1)} %fusion), channel_id=1, source_target_pairs={{0,28},{1,29},{2,30},{3,31},{4,32},{5,33},{6,34},{7,35},{8,36},{9,... | collective-permute-start | bytes 147464
  1281.2 98.0 %collective-permute-start.38 = (f32[8,1536]{1,0:T(8,128)S(1)}, f32[8,1536]{1,0:T(8,128)}, u32[]{:S(2)}, u32[]{:S(2)}) collective-permute-start(f32[8,1536]{1,0:T(8,128)S(1)} %fusion), channel_id=1, source_target_pairs={{0,29},{1,30},{2,31},{3,32},{4,33},{5,34},{6,35},{7,36},{8,37},{9,... | collective-permute-start | bytes 147464
  1294.4 87.9 %collective-permute-start.39 = (f32[8,1536]{1,0:T(8,128)S(1)}, f32[8,1536]{1,0:T(8,128)}, u32[]{:S(2)}, u32[]{:S(2)}) collective-permute-start(f32[8,1536]{1,0:T(8,128)S(1)} %fusion), channel_id=1, source_target_pairs={{0,30},{1,31},{2,32},{3,33},{4,34},{5,35},{6,36},{7,37},{8,38},{9,... | collective-permute-start | bytes 147464
  1307.5 84.3 %collective-permute-start.40 = (f32[8,1536]{1,0:T(8,128)S(1)}, f32[8,1536]{1,0:T(8,128)}, u32[]{:S(2)}, u32[]{:S(2)}) collective-permute-start(f32[8,1536]{1,0:T(8,128)S(1)} %fusion), channel_id=1, source_target_pairs={{0,31},{1,32},{2,33},{3,34},{4,35},{5,36},{6,37},{7,38},{8,39},{9,... | collective-permute-start | bytes 147464
  1315.9 78.8 %collective-permute-start.41 = (f32[8,1536]{1,0:T(8,128)S(1)}, f32[8,1536]{1,0:T(8,128)}, u32[]{:S(2)}, u32[]{:S(2)}) collective-permute-start(f32[8,1536]{1,0:T(8,128)S(1)} %fusion), channel_id=1, source_target_pairs={{0,32},{1,33},{2,34},{3,35},{4,36},{5,37},{6,38},{7,39},{8,40},{9,... | collective-permute-start | bytes 147464
  1466.4 252.4 %collective-permute-start.8 = (bf16[2,256,1536]{1,2,0:T(8,128)(2,1)}, bf16[2,256,1536]{1,2,0:T(8,128)(2,1)}, u32[]{:S(2)}, u32[]{:S(2)}) collective-permute-start(bf16[2,256,1536]{1,2,0:T(8,128)(2,1)} %pad_maximum_fusion.1), channel_id=1, source_target_pairs={{1,0},{2,1},{3,2},{4,3},{5,4},{6,5},{7,6},{8,7},{9,8},{10,9},{11,1... | collective-permute-start | bytes 4718600 | tf_op jit(solution)/shard_map/ppermute | solution.py:26
  1469.0 251.5 %collective-permute-start.9 = (bf16[2,256,1536]{1,2,0:T(8,128)(2,1)}, bf16[2,256,1536]{1,2,0:T(8,128)(2,1)}, u32[]{:S(2)}, u32[]{:S(2)}) collective-permute-start(bf16[2,256,1536]{1,2,0:T(8,128)(2,1)} %pad_maximum_fusion.2), channel_id=1, source_target_pairs={{0,1},{1,2},{2,3},{3,4},{4,5},{5,6},{6,7},{7,8},{8,9},{9,10},{10,1... | collective-permute-start | bytes 4718600 | tf_op jit(solution)/shard_map/ppermute | solution.py:26
  (209 other events, 11220.4 us)
Sparse Core Ops, SparseCore 0:
  1476.9 240.1 all-reduce.3
where the time goes:
time: 1750 us; the launch traced here: 1730 us
  blocking collectives  723 us (41%)
  starting transfers between devices  543 us (31%)
  local copies, waits for them, and re-layouts  176 us (10%)
  waiting for transfers between devices  133 us (8%)
  other arithmetic  95.4 us (5%)
  matrix products  43.9 us (3%)
  between operations  17.7 us (1%)
    unnamed x1, blocking collectives  723 us
    unnamed x64, starting transfers between devices  491 us
    psum x1, waiting for transfers between devices, per_device(): grad_kernel = lax.psum(jnp.stack(kernel_rows), ('dp', 'seq')) * scale_out  129 us
    unnamed x323, local copies, waits for them, and re-layouts  104 us
    reduce_sum x6, other arithmetic, per_device(): jnp.sum(jnp.where(masks[offset], conv_grad_f * attended_wide[offset:offse...  40.2 us
  transfers between devices with their start and end apart: 75, of which 3 were waited for; matrix products, arithmetic and copies ran while one was open for 11% of the time, Pallas kernels for 0%

commit v1 on v0

--- a/solution.py
+++ b/solution.py
@@ -145,7 +145,8 @@
             )
         )
     scale_out = (lax.axis_size("dp") * lax.axis_size("seq") * frame_count) ** (-0.5)
-    grad_kernel = lax.psum(jnp.stack(kernel_rows), ("dp", "seq")) * scale_out
+    cut_the_quotas = lambda vals: jnp.sum(jax.lax.all_gather(vals, axis_name=("dp", "seq")), axis=0)
+    grad_kernel = cut_the_quotas(jnp.stack(kernel_rows)) * scale_out
     attended_grad_b = attended_grad.astype(jnp.bfloat16)
     reduced = lax.psum_scatter(
         lax.dot_general(

time: 1750 us -> 1680 us (0.960)
  waiting for transfers between devices: 133 us -> 3.79 us
  starting transfers between devices: 543 us -> 571 us
    psum x1 -> x0, waiting for transfers between devices: 129 us -> none  [per_device(): grad_kernel = lax.psum(jnp.stack(kernel_rows), ('dp', 'seq')) * scale_out]
    unnamed x64, starting transfers between devices: 491 us -> 518 us
    reduce_sum x0 -> x1, other arithmetic: none -> 17.7 us  [per_device(): jnp.sum(jax.lax.all_gather(vals, axis_name=('dp', 'seq')), axis=0)]
    unnamed x323 -> x205, local copies, waits for them, and re-layouts: 104 us -> 105 us
  transfers between devices with their start and end apart: 75 -> 75, of which waited for: 3 -> 3; matrix products, arithmetic and copies ran while one was open for 11% -> 57% of each run, Pallas kernels for 0% -> 0%
where the time goes in v1:
time: 1680 us; the launch traced here: 1660 us
  blocking collectives  738 us (44%)
  starting transfers between devices  571 us (34%)
  local copies, waits for them, and re-layouts  183 us (11%)
  other arithmetic  108 us (6%)
  matrix products  43.8 us (3%)
  between operations  17.1 us (1%)
    unnamed x1, blocking collectives  738 us
    unnamed x64, starting transfers between devices  518 us
    unnamed x205, local copies, waits for them, and re-layouts  105 us
    reduce_sum x6, other arithmetic, per_device(): jnp.sum(jnp.where(masks[offset], conv_grad_f * attended_wide[offset:offse...  37.2 us
  transfers between devices with their start and end apart: 75, of which 3 were waited for; matrix products, arithmetic and copies ran while one was open for 57% of the time, Pallas kernels for 0%

profile of v1, /device:TPU:1, one launch (start us, length us, event | category | flops | bytes accessed | tf_op | source)
XLA Modules:
  0.0 1664.8 jit_solution(14681811792974345620)
XLA Ops:
  56.4 32.8 %while.30 = (s32[]{:T(128)}, f32[6,256,256]{1,2,0:T(8,128)}, f32[6,4,256]{2,1,0:T(4,128)}, f32[6,4,256]{2,1,0:T(4,128)}, bf16[6,768,256]{1,2,0:T(8,128)(2,1)S(1)...) while((s32[]{:T(128)}, f32[6,256,256]{1,2,0:T(8,128)}, ...), condition=%wide.region_3.4_spmd.clone, body=%wide.region_0.3_spmd.sunk.clone | while | flops 210958336 | bytes 13803641 | solution.py:104
  101.9 22.1 %fusion.142 = (f32[1536]{0:T(1024)S(1)}, f32[1536]{0:T(1024)S(1)}, f32[1536]{0:T(1024)S(1)}, f32[1536]{0:T(1024)S(1)}, f32[1536]{0:T(1024)S(1)}, /*index=5*/f32[...) fusion(pred[256]{0:T(512)(128)(4,1)S(1)} %get-tuple-element.289, ...), kind=kLoop, calls=%fused_computation.286 | loop fusion | flops 104193024 | bytes 4259328 | tf_op jit(solution)/shard_map/reduce_sum | solution.py:138
  161.6 23.9 %fusion.149 = bf16[256,1536]{1,0:T(8,128)(2,1)S(1)} fusion(bf16[256,1536]{1,0:T(8,128)(2,1)S(1)} %get-tuple-element.248, bf16[15,1536]{1,0:T(8,128)(2,1)} %collective-permute-done.7, bf16[15,1536]{1,0:T(8,128)(2,1)} %collective-permute-done.6, f32[1536]{0:T(1024)S(1)} %get-tuple-element.174, f32[1536]{0:T(1024)S(1)} %get-tuple-element.175, ...), kind=kLoop, calls=%fused_computation.304 | loop fusion | flops 83755008 | bytes 1863168 | tf_op jit(solution)/shard_map/convert_element_type | solution.py:150
  191.4 737.7 %fusion = f32[8,1536]{1,0:T(8,128)S(1)} fusion(f32[1536,1536]{1,0:T(8,128)} %fusion.216), kind=kCustom, calls=%all-reduce-scatter | all-reduce-scatter fusion | flops 3145729 | bytes 9486336
  943.5 55.6 %while.31 = (s32[]{:T(128)}, bf16[6,256,256]{1,2,0:T(8,128)(2,1)}, f32[6,768,256]{1,2,0:T(8,128)}, f32[6,768,256]{1,2,0:T(8,128)}, bf16[6,768,256]{1,2,0:T(8,128...) while((s32[]{:T(128)}, bf16[6,256,256]{1,2,0:T(8,128)(2,1)}, ...), condition=%wide.region_6.7_spmd.clone, body=%wide.region_5.6_spmd.sunk.clone | while | flops 510590976 | bytes 23503008 | solution.py:175
  1045.1 23.1 %collective-permute-start.56 = (f32[8,1536]{1,0:T(8,128)S(1)}, f32[8,1536]{1,0:T(8,128)S(1)}, u32[]{:S(2)}, u32[]{:S(2)}) collective-permute-start(f32[8,1536]{1,0:T(8,128)S(1)} %fusion), channel_id=1, source_target_pairs={{0,47},{1,48},{2,49},{3,50},{4,51},{5,52},{6,53},{7,54},{8,55},{9,... | collective-permute-start | bytes 147464
  1144.8 13.1 collective-permute-start.38
  1158.0 13.1 collective-permute-start.37
  1171.1 13.1 collective-permute-start.36
  1184.3 13.1 collective-permute-start.35
  1197.4 13.1 collective-permute-start.34
  1210.6 13.1 collective-permute-start.33
  1223.7 13.1 collective-permute-start.32
  1236.9 13.1 collective-permute-start.31
  1250.0 13.1 collective-permute-start.30
  1263.2 13.1 collective-permute-start.29
  1276.3 13.1 collective-permute-start.28
  1447.3 13.7 collective-permute-start.15
  1461.0 13.1 collective-permute-start.14
  1474.2 13.2 collective-permute-start.13
  1487.7 13.2 collective-permute-start.12
  1500.8 13.1 collective-permute-start.11
  1534.0 97.0 %concatenate.118 = f32[518,1536]{1,0:T(8,128)} concatenate(f32[6,1536]{1,0:T(8,128)S(1)} %collective-permute-done.73, f32[8,1536]{1,0:T(8,128)S(1)} %collective-permute-done.72, f32[8,1536]{1,0:T(8,128)S(1)} %collective-permute-done.71, f32[8,1536]{1,0:T(8,128)S(1)} %collective-permute-done.70, f32[8,1536]{1,0:T(8,128)S(1)} %collective-permute-done.69, ...), dimensions={0} | concatenate | bytes 6365184
  1639.4 17.7 %reduce_sum.338 = f32[31,1536]{1,0:T(8,128)S(1)} reduce(f32[256,31,1536]{2,1,0:T(8,128)} %all-gather.4.cloned.1.call-done, f32[]{:T(128)} %constant.56.clone.1), dimensions={0}, to_apply=%region_38.39 | reduce | flops 12142080 | bytes 48949252 | tf_op jit(solution)/shard_map/reduce_sum | solution.py:148
  (547 shorter events, 515.0 us)
Async XLA Ops:
  7.2 1632.2 %all-gather.4.cloned.1.call-start = ((), (), s32[]{:S(2)}) async-start(), calls=%async_computation | async-start | bytes 50528256 | tf_op jit(solution)/shard_map/all_gather | solution.py:148
  929.1 75.8 %collective-permute-start.72 = (f32[8,1536]{1,0:T(8,128)S(1)}, f32[8,1536]{1,0:T(8,128)S(1)}, u32[]{:S(2)}, u32[]{:S(2)}) collective-permute-start(f32[8,1536]{1,0:T(8,128)S(1)} %fusion), channel_id=1, source_target_pairs={{0,63},{1,64},{2,65},{3,66},{4,67},{5,68},{6,69},{7,70},{8,71},{9,... | collective-permute-start | bytes 147464
  930.4 75.8 %collective-permute-start.71 = (f32[8,1536]{1,0:T(8,128)S(1)}, f32[8,1536]{1,0:T(8,128)S(1)}, u32[]{:S(2)}, u32[]{:S(2)}) collective-permute-start(f32[8,1536]{1,0:T(8,128)S(1)} %fusion), channel_id=1, source_target_pairs={{0,62},{1,63},{2,64},{3,65},{4,66},{5,67},{6,68},{7,69},{8,70},{9,... | collective-permute-start | bytes 147464
  931.7 77.2 %collective-permute-start.70 = (f32[8,1536]{1,0:T(8,128)S(1)}, f32[8,1536]{1,0:T(8,128)S(1)}, u32[]{:S(2)}, u32[]{:S(2)}) collective-permute-start(f32[8,1536]{1,0:T(8,128)S(1)} %fusion), channel_id=1, source_target_pairs={{0,61},{1,62},{2,63},{3,64},{4,65},{5,66},{6,67},{7,68},{8,69},{9,... | collective-permute-start | bytes 147464
  933.0 77.2 %collective-permute-start.69 = (f32[8,1536]{1,0:T(8,128)S(1)}, f32[8,1536]{1,0:T(8,128)S(1)}, u32[]{:S(2)}, u32[]{:S(2)}) collective-permute-start(f32[8,1536]{1,0:T(8,128)S(1)} %fusion), channel_id=1, source_target_pairs={{0,60},{1,61},{2,62},{3,63},{4,64},{5,65},{6,66},{7,67},{8,68},{9,... | collective-permute-start | bytes 147464
  940.4 63.3 %collective-permute-start.73 = (f32[6,1536]{1,0:T(8,128)S(1)}, f32[6,1536]{1,0:T(8,128)S(1)}, u32[]{:S(2)}, u32[]{:S(2)}) collective-permute-start(f32[6,1536]{1,0:T(8,128)S(1)} %slice.909), channel_id=1, source_target_pairs={{0,64},{1,65},{2,66},{3,67},{4,68},{5,69},{6,70},{7,71},{8,72},{9,... | collective-permute-start | bytes 110600
  1016.7 615.9 %collective-permute-start.9 = (bf16[2,256,1536]{1,2,0:T(8,128)(2,1)}, bf16[2,256,1536]{1,2,0:T(8,128)(2,1)}, u32[]{:S(2)}, u32[]{:S(2)}) collective-permute-start(bf16[2,256,1536]{1,2,0:T(8,128)(2,1)} %pad_maximum_fusion.2), channel_id=1, source_target_pairs={{0,1},{1,2},{2,3},{3,4},{4,5},{5,6},{6,7},{7,8},{8,9},{9,10},{10,1... | collective-permute-start | bytes 4718600 | tf_op jit(solution)/shard_map/ppermute | solution.py:26
  1018.8 615.5 %collective-permute-start.8 = (bf16[2,256,1536]{1,2,0:T(8,128)(2,1)}, bf16[2,256,1536]{1,2,0:T(8,128)(2,1)}, u32[]{:S(2)}, u32[]{:S(2)}) collective-permute-start(bf16[2,256,1536]{1,2,0:T(8,128)(2,1)} %pad_maximum_fusion.1), channel_id=1, source_target_pairs={{1,0},{2,1},{3,2},{4,3},{5,4},{6,5},{7,6},{8,7},{9,8},{10,9},{11,1... | collective-permute-start | bytes 4718600 | tf_op jit(solution)/shard_map/ppermute | solution.py:26
  1026.7 41.5 %collective-permute-start.58 = (f32[8,1536]{1,0:T(8,128)S(1)}, f32[8,1536]{1,0:T(8,128)S(1)}, u32[]{:S(2)}, u32[]{:S(2)}) collective-permute-start(f32[8,1536]{1,0:T(8,128)S(1)} %fusion), channel_id=1, source_target_pairs={{0,49},{1,50},{2,51},{3,52},{4,53},{5,54},{6,55},{7,56},{8,57},{9,... | collective-permute-start | bytes 147464
  1144.8 39.4 %collective-permute-start.38 = (f32[8,1536]{1,0:T(8,128)S(1)}, f32[8,1536]{1,0:T(8,128)S(1)}, u32[]{:S(2)}, u32[]{:S(2)}) collective-permute-start(f32[8,1536]{1,0:T(8,128)S(1)} %fusion), channel_id=1, source_target_pairs={{0,29},{1,30},{2,31},{3,32},{4,33},{5,34},{6,35},{7,36},{8,37},{9,... | collective-permute-start | bytes 147464
  1158.0 39.4 %collective-permute-start.37 = (f32[8,1536]{1,0:T(8,128)S(1)}, f32[8,1536]{1,0:T(8,128)S(1)}, u32[]{:S(2)}, u32[]{:S(2)}) collective-permute-start(f32[8,1536]{1,0:T(8,128)S(1)} %fusion), channel_id=1, source_target_pairs={{0,28},{1,29},{2,30},{3,31},{4,32},{5,33},{6,34},{7,35},{8,36},{9,... | collective-permute-start | bytes 147464
  1171.1 39.4 %collective-permute-start.36 = (f32[8,1536]{1,0:T(8,128)S(1)}, f32[8,1536]{1,0:T(8,128)S(1)}, u32[]{:S(2)}, u32[]{:S(2)}) collective-permute-start(f32[8,1536]{1,0:T(8,128)S(1)} %fusion), channel_id=1, source_target_pairs={{0,27},{1,28},{2,29},{3,30},{4,31},{5,32},{6,33},{7,34},{8,35},{9,... | collective-permute-start | bytes 147464
  1184.3 39.4 %collective-permute-start.35 = (f32[8,1536]{1,0:T(8,128)S(1)}, f32[8,1536]{1,0:T(8,128)S(1)}, u32[]{:S(2)}, u32[]{:S(2)}) collective-permute-start(f32[8,1536]{1,0:T(8,128)S(1)} %fusion), channel_id=1, source_target_pairs={{0,26},{1,27},{2,28},{3,29},{4,30},{5,31},{6,32},{7,33},{8,34},{9,... | collective-permute-start | bytes 147464
  1197.4 39.4 %collective-permute-start.34 = (f32[8,1536]{1,0:T(8,128)S(1)}, f32[8,1536]{1,0:T(8,128)S(1)}, u32[]{:S(2)}, u32[]{:S(2)}) collective-permute-start(f32[8,1536]{1,0:T(8,128)S(1)} %fusion), channel_id=1, source_target_pairs={{0,25},{1,26},{2,27},{3,28},{4,29},{5,30},{6,31},{7,32},{8,33},{9,... | collective-permute-start | bytes 147464
  1210.6 39.4 %collective-permute-start.33 = (f32[8,1536]{1,0:T(8,128)S(1)}, f32[8,1536]{1,0:T(8,128)S(1)}, u32[]{:S(2)}, u32[]{:S(2)}) collective-permute-start(f32[8,1536]{1,0:T(8,128)S(1)} %fusion), channel_id=1, source_target_pairs={{0,24},{1,25},{2,26},{3,27},{4,28},{5,29},{6,30},{7,31},{8,32},{9,... | collective-permute-start | bytes 147464
  1223.7 39.4 %collective-permute-start.32 = (f32[8,1536]{1,0:T(8,128)S(1)}, f32[8,1536]{1,0:T(8,128)S(1)}, u32[]{:S(2)}, u32[]{:S(2)}) collective-permute-start(f32[8,1536]{1,0:T(8,128)S(1)} %fusion), channel_id=1, source_target_pairs={{0,23},{1,24},{2,25},{3,26},{4,27},{5,28},{6,29},{7,30},{8,31},{9,... | collective-permute-start | bytes 147464
  1236.9 39.4 %collective-permute-start.31 = (f32[8,1536]{1,0:T(8,128)S(1)}, f32[8,1536]{1,0:T(8,128)S(1)}, u32[]{:S(2)}, u32[]{:S(2)}) collective-permute-start(f32[8,1536]{1,0:T(8,128)S(1)} %fusion), channel_id=1, source_target_pairs={{0,22},{1,23},{2,24},{3,25},{4,26},{5,27},{6,28},{7,29},{8,30},{9,... | collective-permute-start | bytes 147464
  1250.0 39.4 %collective-permute-start.30 = (f32[8,1536]{1,0:T(8,128)S(1)}, f32[8,1536]{1,0:T(8,128)S(1)}, u32[]{:S(2)}, u32[]{:S(2)}) collective-permute-start(f32[8,1536]{1,0:T(8,128)S(1)} %fusion), channel_id=1, source_target_pairs={{0,21},{1,22},{2,23},{3,24},{4,25},{5,26},{6,27},{7,28},{8,29},{9,... | collective-permute-start | bytes 147464
  1421.0 40.0 %collective-permute-start.17 = (f32[8,1536]{1,0:T(8,128)S(1)}, f32[8,1536]{1,0:T(8,128)S(1)}, u32[]{:S(2)}, u32[]{:S(2)}) collective-permute-start(f32[8,1536]{1,0:T(8,128)S(1)} %fusion), channel_id=1, source_target_pairs={{0,8},{1,9},{2,10},{3,11},{4,12},{5,13},{6,14},{7,15},{8,16},{9,17... | collective-permute-start | bytes 147464
  1434.1 40.0 %collective-permute-start.16 = (f32[8,1536]{1,0:T(8,128)S(1)}, f32[8,1536]{1,0:T(8,128)S(1)}, u32[]{:S(2)}, u32[]{:S(2)}) collective-permute-start(f32[8,1536]{1,0:T(8,128)S(1)} %fusion), channel_id=1, source_target_pairs={{0,7},{1,8},{2,9},{3,10},{4,11},{5,12},{6,13},{7,14},{8,15},{9,16}... | collective-permute-start | bytes 147464
  1447.3 40.4 %collective-permute-start.15 = (f32[8,1536]{1,0:T(8,128)S(1)}, f32[8,1536]{1,0:T(8,128)}, u32[]{:S(2)}, u32[]{:S(2)}) collective-permute-start(f32[8,1536]{1,0:T(8,128)S(1)} %fusion), channel_id=1, source_target_pairs={{0,6},{1,7},{2,8},{3,9},{4,10},{5,11},{6,12},{7,13},{8,14},{9,15},... | collective-permute-start | bytes 147464
  1461.0 39.8 %collective-permute-start.14 = (f32[8,1536]{1,0:T(8,128)S(1)}, f32[8,1536]{1,0:T(8,128)}, u32[]{:S(2)}, u32[]{:S(2)}) collective-permute-start(f32[8,1536]{1,0:T(8,128)S(1)} %fusion), channel_id=1, source_target_pairs={{0,5},{1,6},{2,7},{3,8},{4,9},{5,10},{6,11},{7,12},{8,13},{9,14},{... | collective-permute-start | bytes 147464
  1474.2 39.8 %collective-permute-start.13 = (f32[8,1536]{1,0:T(8,128)S(1)}, f32[8,1536]{1,0:T(8,128)}, u32[]{:S(2)}, u32[]{:S(2)}) collective-permute-start(f32[8,1536]{1,0:T(8,128)S(1)} %fusion), channel_id=1, source_target_pairs={{0,4},{1,5},{2,6},{3,7},{4,8},{5,9},{6,10},{7,11},{8,12},{9,13},{1... | collective-permute-start | bytes 147464
  1487.7 46.2 %collective-permute-start.12 = (f32[8,1536]{1,0:T(8,128)S(1)}, f32[8,1536]{1,0:T(8,128)}, u32[]{:S(2)}, u32[]{:S(2)}) collective-permute-start(f32[8,1536]{1,0:T(8,128)S(1)} %fusion), channel_id=1, source_target_pairs={{0,3},{1,4},{2,5},{3,6},{4,7},{5,8},{6,9},{7,10},{8,11},{9,12},{10... | collective-permute-start | bytes 147464
  (150 other events, 12708.3 us)
Sparse Core Ops, SparseCore 0:
  151.9 197.1 all-gather.3
